TPU v7x, 256 devices: a whole 4x4x8 slice. The times are simulated.
256 devices in a mesh: illum: 8 (over z), box: 32 (over x, y, core).
Axes of the slice: x: 4, y: 4, z: 8, core: 2. Of those that a mesh axis runs over, the one named last changes fastest.
Arguments:
- patterns: bfloat16 [2, 512, 128, 1024], P(None, 'box', None, 'illum'), parts along dimension 3, may hold values from -6 to 6
- owner_block: int32 [4], replicated, may hold values from 0 to 63
- low_index: int32 [512, 48], P('box'), may hold values from 0 to 315
- low_mask: int32 [512, 48], P('box'), may hold values 0 or 1
- low_table: bfloat16 [2, 316, 128], replicated, may hold values from -2 to 2
- interp: bfloat16 [128, 512], replicated, may hold values from -0.5 to 0.5
- shift_angle: float32 [8, 512], replicated, may hold values from -3.140625 to 3.140625
- par_source: int32 [64, 16], replicated, may hold values from 0 to 63, as said below
- par_index: int32 [64, 16], replicated, may hold values from 0 to 315
- par_mask: int32 [64, 16], replicated, may hold values 0 or 1
- par_table: bfloat16 [2, 316, 512], replicated, may hold values from -1.5 to 1.5
Outputs:
- incoming: float32 [2, 512, 128, 1024], P(None, 'box', None, 'illum'), parts along dimension 3
There are 8 independent parts, one for each index of `illum`. A program takes and returns all parts, laid end to end along the dimension named above; an argument that names none is the same for every part. Nothing has to cross between parts.
Inputs may be any that keep to these rules, and one draw needn't show every extreme that they name: `par_source`: each parent's 16 slots name distinct parents other than itself.
All inputs are finite; a program needn't handle non-finite values. No bound on the sum of `low_mask` on one device may be relied on, other than what follows from the above.
Results may differ from a plain program's by a relative error of at most 0.0047.
Values may be sent and summed in bfloat16 or wider, within the bound.
No kernel may reach another device: no remote copies, remote signals or barrier semaphores. Data moves between devices by JAX's collectives and lax.ppermute only.
A program may use at most 64 MiB of HBM per device.

v0:
```python
import functools

import jax
import jax.numpy as jnp
from jax import lax
from jax.experimental import pallas as pl
from jax.experimental.pallas import tpu as pltpu
from jax.sharding import PartitionSpec as P

F32 = jnp.float32
BF16 = jnp.bfloat16
LANES = 128
LIMIT = 40 * 1024 * 1024
FULL = 60 * 1024 * 1024
GROUP = 2
DEV = 32
BOX = 16
K = 128
Q = 512
R = 128
QS = Q // DEV
KS = K // DEV
NPAD = 384
FAR = 32
L_ROWS = 4 * QS
P_ROWS = 2 * KS * 8
T_ROWS = BOX
SEND1 = L_ROWS + P_ROWS + T_ROWS
N_ROWS = 2 * KS * BOX
SEND2 = L_ROWS + N_ROWS


def iota(shape, dim):
    return lax.broadcasted_iota(jnp.int32, shape, dim)


def pick(row, index, chunk):
    total = None
    for part in range(NPAD // LANES):
        source = jnp.broadcast_to(row(part), index.shape)
        got = jnp.take_along_axis(source, index, axis=1, mode="promise_in_bounds")
        total = got if total is None else jnp.where(chunk == part, got, total)
    return total


def split(out_ref, c, rows):
    for part in range(NPAD // LANES):
        out_ref[c, part] = rows[:, part * LANES : (part + 1) * LANES]


def transpose_table(table_ref, out_ref):
    count = table_ref.shape[1]
    for part in range(2):
        wide = table_ref[part].astype(F32)
        wide = jnp.concatenate([wide, jnp.zeros((NPAD - count, wide.shape[1]), F32)], axis=0)
        split(out_ref, part, jnp.transpose(wide))


def first_parity(owner, device):
    result = jnp.int32(0)
    for step in reversed(range(owner.shape[0])):
        value = owner[step]
        result = jnp.where((value >> 1) == device, value & 1, result)
    return result


def widen(patterns, wide, parity):
    for c in range(2):
        for i in range(8):
            wide[c, i * K : (i + 1) * K, :] = patterns[c, parity * 8 + i].astype(F32)


def cut(out, base, wide, devices):
    for d in devices:
        for c in range(2):
            for half in range(KS // 2):
                pieces = [wide[c, pl.ds(d * KS + 2 * half + k, 8, stride=K), :] for k in range(2)]
                at = base + c * KS * 8 + half * 16
                out[d, at : at + 16, :] = jnp.concatenate(pieces, axis=0).astype(BF16)


def start_all(pairs, sems):
    copies = [pltpu.make_async_copy(*pair, sems.at[i]) for i, pair in enumerate(pairs)]
    for copy in copies:
        copy.start()
    return copies


def up_kernel(
    owner_in, patterns_in, index_in, mask_in, interp_in, angle_in, send_out,
    owner, patterns, index, mask, interp, angle, sems, weights, fields, wide, spread, send, out_sems,
):
    copies = start_all(
        (
            (interp_in, interp),
            (angle_in, angle),
            (patterns_in, patterns),
            (owner_in, owner),
            (index_in, index),
            (mask_in, mask),
        ),
        sems,
    )
    me = lax.axis_index("box")
    copies[0].wait()
    copies[1].wait()
    smooth = interp[...].astype(F32)
    cosine, sine = jnp.cos(angle[...]), jnp.sin(angle[...])
    for b in range(8):
        rows = 2 * b * K
        weights[rows : rows + K, :] = (smooth * cosine[b : b + 1, :]).astype(BF16)
        weights[rows + K : rows + 2 * K, :] = (smooth * sine[b : b + 1, :]).astype(BF16)
    for copy in copies[2:]:
        copy.wait()
    for b in range(8):
        rows = 2 * b * K
        for p in range(2):
            real, imag = patterns[0, 8 * p + b], patterns[1, 8 * p + b]
            fields[rows : rows + K, p * R : (p + 1) * R] = real
            fields[rows + K : rows + 2 * K, p * R : (p + 1) * R] = -imag
            fields[rows : rows + K, (2 + p) * R : (3 + p) * R] = imag
            fields[rows + K : rows + 2 * K, (2 + p) * R : (3 + p) * R] = real
    first = first_parity(owner, me)
    widen(patterns, wide, first)

    spread[:, 0 : index.shape[1]] = jnp.where(mask[...] > 0, index[...], NPAD - 1)
    lane = iota((BOX, LANES), 1)
    number = jnp.take_along_axis(
        spread[...], BOX + (lane & (FAR - 1)), axis=1, mode="promise_in_bounds"
    )
    chunk = number >> 7
    scale = jnp.where(chunk == 0, 1.0, jnp.where(chunk == 1, 256.0, 65536.0)).astype(F32)
    code = ((number & (LANES - 1)) + 128).astype(F32) * scale
    quarter = BOX // 4
    packed = code[0:quarter]
    for group in range(1, 4):
        packed = jnp.where(
            lane[0:quarter] >> 5 == group, code[group * quarter : (group + 1) * quarter], packed
        )
    rows = jnp.concatenate([packed] * 4, axis=0).astype(BF16)
    tile = 256
    ways = tile // QS
    outs = []
    for t in range(Q // tile):
        total = lax.dot_general(
            weights[:, t * tile : (t + 1) * tile],
            fields[...],
            (((0,), (0,)), ((), ())),
            preferred_element_type=F32,
        ).astype(BF16)
        here = range(t * ways, (t + 1) * ways)
        cut(send, L_ROWS, wide, here)
        for d in here:
            send[d, L_ROWS + P_ROWS : SEND1, :] = rows
        for cp in range(4):
            send[t * ways : (t + 1) * ways, cp * QS : (cp + 1) * QS, :] = total[
                :, cp * R : (cp + 1) * R
            ].reshape(ways, QS, R)
        piece = pl.ds(t * ways, ways)
        outs.append(pltpu.make_async_copy(send.at[piece], send_out.at[piece], out_sems.at[t]))
        outs[-1].start()
    for copy in outs:
        copy.wait()


def side_kernel(
    owner, patterns_in, index_in, mask_in, table_in, par_source_in, par_index_in, par_mask_in,
    par_table_in, interp_in, angle_in,
    near_out, coupling_out, own_table_out, weights_out, extra_out,
    patterns, index, mask, table, par_source, par_index, par_mask, par_table, interp, angle, sems,
    near, coupling, own_table, weights, extra, out_sems,
    wide, table_t, par_t, spread, par_rows, block,
):
    copies = start_all(
        (
            (table_in, table),
            (par_table_in, par_table),
            (patterns_in, patterns),
            (index_in, index),
            (mask_in, mask),
            (par_source_in, par_source),
            (par_index_in, par_index),
            (par_mask_in, par_mask),
            (interp_in, interp),
            (angle_in, angle),
        ),
        sems,
    )
    me = lax.axis_index("box")
    twice = jnp.int32(0)
    for i in range(owner.shape[0]):
        for j in range(i):
            same = (owner[i] >> 1) == (owner[j] >> 1)
            twice = jnp.where(same & (owner[i] != owner[j]), 1, twice)

    for copy in copies:
        copy.wait()
    transpose_table(table, table_t)
    for c in range(2):
        for part in range(NPAD // LANES):
            for k in range(KS):
                own_table[c, part, k : k + 1, :] = table_t[c, part, pl.ds(me * KS + k, 1), :]

    @pl.when(twice > 0)
    def _():
        widen(patterns, block, 1 - first_parity(owner, me))
        cut(extra, 0, block, range(DEV))
        copy = pltpu.make_async_copy(extra, extra_out, out_sems.at[4])
        copy.start()
        copy.wait()

    chosen = (iota((QS, Q), 1) == me * QS + iota((QS, Q), 0)).astype(BF16)
    count = par_table.shape[1]
    for c in range(2):
        rows = lax.dot_general(
            chosen, par_table[c], (((1,), (1,)), ((), ())), preferred_element_type=F32
        )
        split(par_t, c, jnp.concatenate([rows, jnp.zeros((QS, NPAD - count), F32)], axis=1))
    slots, parents = par_source.shape
    here = iota((LANES, LANES), 0)
    source_here = (here & (DEV - 1)) * 2 + ((here >> 5) & 1)
    par_rows[0, 0:slots, 0:parents] = par_source[...].astype(F32)
    par_rows[1, 0:slots, 0:parents] = jnp.where(
        par_mask[...] > 0, par_index[...], NPAD - 1
    ).astype(F32)
    wanted = source_here.astype(F32)
    table_at = jnp.full((LANES, LANES), NPAD - 1, F32)
    for j in range(slots):
        table_at = jnp.where(
            par_rows[0, j : j + 1, :] == wanted, par_rows[1, j : j + 1, :], table_at
        )
    par_rows[0] = jnp.transpose(table_at)
    number = jnp.concatenate(
        [par_rows[0, pl.ds(p, DEV, stride=2), :] for p in range(2)], axis=0
    ).astype(jnp.int32)
    par_low, par_chunk = number & (LANES - 1), number >> 7
    par_imaginary = iota((parents, LANES), 1) >= parents
    for q in range(QS):
        got = [
            pick(lambda part: par_t[c, part, q : q + 1, :], par_low, par_chunk) for c in range(2)
        ]
        coupling[q] = jnp.where(par_imaginary, got[1], got[0]).astype(BF16)
    outs = start_all(((coupling, coupling_out), (own_table, own_table_out)), out_sems)

    cosine, sine = jnp.cos(angle[...]), jnp.sin(angle[...])
    smooth = interp[...].astype(F32)
    for b in range(8):
        weights[b * K : (b + 1) * K, 0:Q] = (smooth * cosine[b : b + 1, :]).astype(BF16)
        weights[b * K : (b + 1) * K, Q : 2 * Q] = (smooth * sine[b : b + 1, :]).astype(BF16)
    outs.append(pltpu.make_async_copy(weights, weights_out, out_sems.at[2]))
    outs[-1].start()

    for c in range(2):
        for b in range(BOX):
            wide[c, b * K : (b + 1) * K, :] = patterns[c, b].astype(F32)
    spread[:, 0 : index.shape[1]] = jnp.where(mask[...] > 0, index[...], NPAD - 1)
    lane = iota((BOX, LANES), 1)
    code = jnp.take_along_axis(spread[...], lane & (BOX - 1), axis=1, mode="promise_in_bounds")
    low, chunk = code & (LANES - 1), code >> 7
    imaginary = ((lane >> 4) & 1) == 1
    zero = jnp.zeros((BOX, LANES), F32)

    for g in range(K // 8):
        left, right = [], []
        for kk in range(8):
            k = g * 8 + kk
            got = [
                pick(lambda part: table_t[c, part, k : k + 1, :], low, chunk) for c in range(2)
            ]
            value = jnp.where(imaginary, got[1], got[0])
            value = jnp.where((lane >> 5) == kk % 4, value, 0.0)
            left.append(
                jnp.concatenate([value, zero] if kk < 4 else [zero, value], axis=1)
            )
            real, imag = [wide[c, pl.ds(k, BOX, stride=K), :] for c in range(2)]
            right.append(doubled(real, imag))
        total = jnp.dot(
            jnp.concatenate(left, axis=0).astype(BF16),
            jnp.concatenate(right, axis=0),
            preferred_element_type=F32,
        )
        for kk in range(8):
            for c in range(2):
                near[c, pl.ds(g * 8 + kk, BOX, stride=K), :] = total[
                    kk * BOX : (kk + 1) * BOX, c * R : (c + 1) * R
                ]
    outs.append(pltpu.make_async_copy(near, near_out, out_sems.at[3]))
    outs[-1].start()
    for copy in outs:
        copy.wait()


def doubled(real, imag):
    return jnp.concatenate(
        [
            jnp.concatenate([real, imag], axis=1),
            jnp.concatenate([-imag, real], axis=1),
        ],
        axis=0,
    ).astype(BF16)


def middle_kernel(
    owner, received, extra, coupling, table, send,
    sems, fields, lifted, moved, codes, there,
):
    def place(s, c, half, piece):
        for k in range(2):
            row = (2 * half + k) * FAR + s * 8
            fields[c, row : row + 8, :] = piece[8 * k : 8 * k + 8].astype(F32)

    pieces = [
        (c, half, c * KS * 8 + half * 16) for c in range(2) for half in range(KS // 2)
    ]
    seconds = []
    for s in range(owner.shape[0]):
        device = owner[s] >> 1
        seconds.append((owner[s] & 1) != first_parity(owner, device))
        for c, half, at in pieces:
            place(s, c, half, received[device, L_ROWS + at : L_ROWS + at + 16, :])

    @pl.when(functools.reduce(jnp.logical_or, seconds))
    def _():
        for s, second in enumerate(seconds):

            @pl.when(second)
            def _():
                for c, half, at in pieces:
                    copy = pltpu.make_async_copy(
                        extra.at[owner[s] >> 1, at : at + 16], there, sems.at[0]
                    )
                    copy.start()
                    copy.wait()
                    place(s, c, half, there[...])

    size = DEV * QS
    for cp in range(4):
        lifted[cp * size : (cp + 1) * size, :] = (
            received[:, cp * QS : (cp + 1) * QS, :].reshape(size, R).astype(F32)
        )
    for q in range(QS):
        parts = [lifted[pl.ds(cp * size + q, DEV, stride=QS), :] for cp in range(4)]
        right = doubled(
            jnp.concatenate(parts[:2], axis=0), jnp.concatenate(parts[2:], axis=0)
        )
        total = jnp.dot(coupling[q], right, preferred_element_type=F32)
        for c in range(2):
            for p in range(2):
                moved[pl.ds((2 * c + p) * size + q, DEV, stride=QS), :] = total[
                    p * DEV : (p + 1) * DEV, c * R : (c + 1) * R
                ]
    for cp in range(4):
        send[:, cp * QS : (cp + 1) * QS, :] = (
            moved[cp * size : (cp + 1) * size, :].reshape(DEV, QS, R).astype(BF16)
        )

    codes[...] = (
        received[:, L_ROWS + P_ROWS : SEND1, :].reshape(DEV * BOX, LANES).astype(F32)
    )
    code = jnp.concatenate([codes[pl.ds(i, DEV, stride=BOX), :] for i in range(4)], axis=0)
    chunk = (code >= 32768.0).astype(jnp.int32) + (code >= 8388608.0).astype(jnp.int32)
    scale = jnp.where(chunk == 0, 1.0, jnp.where(chunk == 1, 1 / 256, 1 / 65536)).astype(F32)
    low = (code * scale).astype(jnp.int32) - 128
    low = low & (LANES - 1)
    lane = iota((4 * DEV, 2 * LANES), 1) & (LANES - 1)
    keeps = [jnp.where(lane >> 5 == group, 1.0, 0.0).astype(BF16) for group in range(4)]
    for k in range(KS):
        got = [
            pick(lambda part: table[c, part, k : k + 1, :], low, chunk) for c in range(2)
        ]
        both = jnp.concatenate(got, axis=1).astype(BF16)
        left = jnp.concatenate([both * keep for keep in keeps], axis=0)
        rows = slice(k * FAR, (k + 1) * FAR)
        right = doubled(
            jnp.concatenate([fields[0, rows, :]] * 4, axis=0),
            jnp.concatenate([fields[1, rows, :]] * 4, axis=0),
        )
        total = jnp.dot(left, right, preferred_element_type=F32)
        for c in range(2):
            for b in range(BOX):
                moved[pl.ds((c * KS + k) * size + b, DEV, stride=BOX), :] = total[
                    b * DEV : (b + 1) * DEV, c * R : (c + 1) * R
                ]
    for ck in range(2 * KS):
        row = L_ROWS + ck * BOX
        send[:, row : row + BOX, :] = (
            moved[ck * size : (ck + 1) * size, :].reshape(DEV, BOX, R).astype(BF16)
        )


def down_kernel(received, near, weights, out, fields, far, result, sems):
    for p in range(2):
        real = received[:, p * QS : (p + 1) * QS, :].reshape(Q, R)
        imag = received[:, (2 + p) * QS : (3 + p) * QS, :].reshape(Q, R)
        fields[0:Q, p * R : (p + 1) * R] = real
        fields[Q : 2 * Q, p * R : (p + 1) * R] = imag
        fields[0:Q, (2 + p) * R : (3 + p) * R] = imag
        fields[Q : 2 * Q, (2 + p) * R : (3 + p) * R] = -real
    for c in range(2):
        row = L_ROWS + c * KS * BOX
        far[c] = received[:, row : row + KS * BOX, :].reshape(K * BOX, R).astype(F32)
    copies = []
    for first in range(0, 8, GROUP):
        total = jnp.dot(
            weights[first * K : (first + GROUP) * K, :], fields[...], preferred_element_type=F32
        )
        for p in range(2):
            for b in range(first, first + GROUP):
                box = 8 * p + b
                for c in range(2):
                    there = far[c, pl.ds(box, K, stride=BOX), :]
                    at = (2 * c + p) * R
                    result[c, box] = (
                        total[(b - first) * K : (b - first + 1) * K, at : at + R]
                        + near[c, box * K : (box + 1) * K, :]
                        + there
                    )
        for p in range(2):
            boxes = pl.ds(8 * p + first, GROUP)
            copy = pltpu.make_async_copy(
                result.at[:, boxes], out.at[:, boxes], sems.at[2 * first + p]
            )
            copy.start()
            copies.append(copy)
    for copy in copies:
        copy.wait()


def in_vmem(count):
    return [pl.BlockSpec(memory_space=pltpu.VMEM)] * count


IN_HBM = pl.BlockSpec(memory_space=pltpu.HBM)
SCALARS = pl.BlockSpec(memory_space=pltpu.SMEM)


def anywhere(count):
    return [pl.BlockSpec(memory_space=pl.ANY)] * count


def params(limit):
    return pltpu.CompilerParams(vmem_limit_bytes=limit)


def shards(
    patterns,
    owner_block,
    low_index,
    low_mask,
    low_table,
    interp,
    shift_angle,
    par_source,
    par_index,
    par_mask,
    par_table,
):
    assert patterns.shape == (2, BOX, K, R) and interp.shape == (K, Q)
    assert lax.axis_size("box") == DEV and low_index.shape == (BOX, BOX + FAR)
    send = pl.pallas_call(
        up_kernel,
        out_shape=jax.ShapeDtypeStruct((DEV, SEND1, R), BF16),
        in_specs=anywhere(6),
        out_specs=IN_HBM,
        scratch_shapes=[
            pltpu.SMEM(owner_block.shape, jnp.int32),
            pltpu.VMEM(patterns.shape, BF16),
            pltpu.VMEM(low_index.shape, jnp.int32),
            pltpu.VMEM(low_mask.shape, jnp.int32),
            pltpu.VMEM(interp.shape, BF16),
            pltpu.VMEM(shift_angle.shape, F32),
            pltpu.SemaphoreType.DMA((6,)),
            pltpu.VMEM((16 * K, Q), BF16),
            pltpu.VMEM((16 * K, 4 * R), BF16),
            pltpu.VMEM((2, 8 * K, R), F32),
            pltpu.VMEM((BOX, LANES), jnp.int32),
            pltpu.VMEM((DEV, SEND1, R), BF16),
            pltpu.SemaphoreType.DMA((5,)),
        ],
        compiler_params=params(FULL),
        cost_estimate=pl.CostEstimate(
            flops=1200000000, bytes_accessed=4000000, transcendentals=8192
        ),
        name="up",
    )(owner_block, patterns, low_index, low_mask, interp, shift_angle)

    received = lax.all_to_all(send, "box", split_axis=0, concat_axis=0, tiled=True)

    made = (
        jax.ShapeDtypeStruct((2, BOX * K, R), F32),
        jax.ShapeDtypeStruct((QS, 2 * DEV, LANES), BF16),
        jax.ShapeDtypeStruct((2, NPAD // LANES, 8, LANES), F32),
        jax.ShapeDtypeStruct((8 * K, 2 * Q), BF16),
        jax.ShapeDtypeStruct((DEV, P_ROWS, R), BF16),
    )
    turned = [jnp.transpose(x) for x in (par_source, par_index, par_mask)]
    near, coupling, own_table, weights, extra = pl.pallas_call(
        side_kernel,
        out_shape=made,
        in_specs=[SCALARS, *anywhere(10)],
        out_specs=(IN_HBM,) * 5,
        scratch_shapes=[
            pltpu.VMEM(patterns.shape, BF16),
            pltpu.VMEM(low_index.shape, jnp.int32),
            pltpu.VMEM(low_mask.shape, jnp.int32),
            pltpu.VMEM(low_table.shape, BF16),
            *[pltpu.VMEM(x.shape, jnp.int32) for x in turned],
            pltpu.VMEM(par_table.shape, BF16),
            pltpu.VMEM(interp.shape, BF16),
            pltpu.VMEM(shift_angle.shape, F32),
            pltpu.SemaphoreType.DMA((10,)),
            *[pltpu.VMEM(x.shape, x.dtype) for x in made],
            pltpu.SemaphoreType.DMA((5,)),
            pltpu.VMEM((2, BOX * K, R), F32),
            pltpu.VMEM((2, NPAD // LANES, K, LANES), F32),
            pltpu.VMEM((2, NPAD // LANES, QS, LANES), F32),
            pltpu.VMEM((BOX, LANES), jnp.int32),
            pltpu.VMEM((2, LANES, LANES), F32),
            pltpu.VMEM((2, 8 * K, R), F32),
        ],
        compiler_params=params(FULL),
        cost_estimate=pl.CostEstimate(
            flops=4000000000, bytes_accessed=12000000, transcendentals=8192
        ),
        name="side",
    )(
        owner_block, patterns, low_index, low_mask, low_table, *turned, par_table, interp,
        shift_angle,
    )

    home, block = owner_block >> 1, owner_block
    twice = jnp.any((home[:, None] == home[None]) & (block[:, None] != block[None]))
    received, extra, twice = lax.optimization_barrier((received, extra, twice))
    extra = lax.cond(
        twice,
        lambda x: lax.all_to_all(x, "box", split_axis=0, concat_axis=0, tiled=True),
        lambda x: x,
        extra,
    )

    size = DEV * QS
    send = pl.pallas_call(
        middle_kernel,
        out_shape=jax.ShapeDtypeStruct((DEV, SEND2, R), BF16),
        in_specs=[SCALARS] + in_vmem(1) + anywhere(1) + in_vmem(2),
        out_specs=in_vmem(1)[0],
        scratch_shapes=[
            pltpu.SemaphoreType.DMA((1,)),
            pltpu.VMEM((2, KS * FAR, R), F32),
            pltpu.VMEM((4 * size, R), F32),
            pltpu.VMEM((2 * KS * size, R), F32),
            pltpu.VMEM((size, LANES), F32),
            pltpu.VMEM((16, R), BF16),
        ],
        compiler_params=params(LIMIT),
        cost_estimate=pl.CostEstimate(
            flops=800000000, bytes_accessed=4000000, transcendentals=0
        ),
        name="middle",
    )(owner_block, received, extra, coupling, own_table)

    received = lax.all_to_all(send, "box", split_axis=0, concat_axis=0, tiled=True)

    return pl.pallas_call(
        down_kernel,
        out_shape=jax.ShapeDtypeStruct((2, BOX, K, R), F32),
        in_specs=in_vmem(3),
        out_specs=IN_HBM,
        scratch_shapes=[
            pltpu.VMEM((2 * Q, 4 * R), BF16),
            pltpu.VMEM((2, K * BOX, R), F32),
            pltpu.VMEM((2, BOX, K, R), F32),
            pltpu.SemaphoreType.DMA((BOX,)),
        ],
        compiler_params=params(LIMIT),
        cost_estimate=pl.CostEstimate(
            flops=1200000000, bytes_accessed=6000000, transcendentals=0
        ),
        name="down",
    )(received, near, weights)


def solution(mesh):
    placed = (
        P(None, "box", None, "illum"),
        P(),
        P("box", None),
        P("box", None),
        P(),
        P(),
        P(),
        P(),
        P(),
        P(),
        P(),
    )
    return jax.shard_map(
        shards, mesh=mesh, in_specs=placed, out_specs=P(None, "box", None, "illum"), check_vma=False
    )
```

profile of v0, /device:TPU:1, one launch (start us, length us, event | category | flops | bytes accessed | tf_op | source)
XLA Modules:
  0.0 64.4 jit_solution(1049972426923013586)
XLA Ops:
  0.0 4.1 %up.1 = bf16[32,144,128]{2,1,0:T(8,128)(2,1)} custom-call(s32[4]{0:T(128)} %owner.3, bf16[2,16,128,128]{3,2,1,0:T(8,128)(2,1)} %patterns_in.3, s32[16,48]{1,0:T(8,128)} %index_in.3, s32[16,48]{1,0:T(8,128)} %mask_in.3, bf16[128,512]{1,0:T(8,128)(2,1)} %interp_in.3, f32[8,512]{1,0:T(8,128)} %angle_in.3), custom_call_target="tpu_custom_call" | custom-call | flops 1200000000 | bytes 4000000 | tf_op jit(solution)/shard_map/up/pallas_call | solution.py:460
  4.1 0.0 copy-start.7
  4.1 0.0 copy-start.6
  4.1 0.0 copy-start.4
  4.1 8.7 %all-to-all-start.1 = ((bf16[32,144,128]{2,1,0:T(8,128)(2,1)}), bf16[32,144,128]{2,1,0:T(8,128)(2,1)S(1)}, u32[]{:S(2)}, u32[]{:S(2)}) async-start(bf16[32,144,128]{2,1,0:T(8,128)(2,1)} %up.1), calls=%async_computation.1 | async-start | bytes 2359296 | tf_op jit(solution)/shard_map/all_to_all | solution.py:487
  12.9 0.0 copy-done.7
  12.9 0.7 %copy.14.table_in = bf16[2,316,128]{2,1,0:T(8,128)(2,1)} copy(bf16[2,316,128]{2,0,1:T(2,128)(2,1)S(1)} %copy-done.7) | data formatting | bytes 323584 | tf_op args[4]
  13.6 0.0 copy-done.6
  13.6 0.9 %copy.15.par_table_in = bf16[2,316,512]{2,1,0:T(8,128)(2,1)} copy(bf16[2,316,512]{2,0,1:T(2,128)(2,1)S(1)} %copy-done.6) | data formatting | bytes 1294336 | tf_op args[10]
  14.5 0.0 copy-done.4
  14.5 0.8 %and_reduce_fusion = pred[]{:T(512)} fusion(s32[4]{0:T(128)S(1)} %copy-done.4, s32[4]{0:T(128)S(1)} %broadcast_shift-right-arithmetic_fusion), kind=kLoop, calls=%fused_computation | loop fusion | flops 63 | bytes 33 | tf_op jit(solution)/shard_map/reduce_or | solution.py:532
  15.3 9.8 %side.1 = (f32[2,2048,128]{2,1,0:T(8,128)}, bf16[16,64,128]{2,1,0:T(8,128)(2,1)}, f32[2,3,8,128]{3,2,1,0:T(8,128)}, bf16[1024,1024]{1,0:T(8,128)(2,1)}, bf16[32,64,128]{2,1,0:T(8,128)(2,1)S(1)}) custom-call(s32[4]{0:T(128)} %owner.3, bf16[2,16,128,128]{3,2,1,0:T(8,128)(2,1)} %patterns_in.3, s32[16,48]{1,0:T(8,128)} %index_in.3, s32[16,48]{1,0:T(8,128)} %mask_in.3, ...), custom_call_target="tpu_custom_call" | custom-call | flops 4000000000 | bytes 12000000 | tf_op jit(solution)/shard_map/side/pallas_call | solution.py:497
  25.0 0.0 copy-start.2
  25.0 0.0 copy-start.3
  25.1 0.0 copy-start.5
  25.1 6.2 %all-to-all-done.1.received = bf16[32,144,128]{2,1,0:T(8,128)(2,1)S(1)} async-done(((bf16[32,144,128]{2,1,0:T(8,128)(2,1)}), bf16[32,144,128]{2,1,0:T(8,128)(2,1)S(1)}, u32[]{:S(2)}, u32[]{:S(2)}) %all-to-all-start.1) | async-done | bytes 1179680 | tf_op jit(solution)/shard_map/all_to_all | solution.py:487
  31.9 0.0 copy-done.2
  31.9 0.0 copy-done.3
  31.9 0.0 copy-done.5
  32.0 0.0 copy-start.1
  32.0 2.7 %middle.1 = bf16[32,192,128]{2,1,0:T(8,128)(2,1)S(1)} custom-call(s32[4]{0:T(128)S(1)} %copy-done.5, bf16[32,144,128]{2,1,0:T(8,128)(2,1)S(1)} %all-to-all-done.1.received, bf16[32,64,128]{2,1,0:T(8,128)(2,1)S(1)} %get-tuple-element.26.extra, bf16[16,64,128]{2,1,0:T(8,128)(2,1)S(1)} %copy-done.2, f32[2,3,8,128]{3,2,1,0:T(8,128)S(1)} %copy-done.3), custom_call_target="tpu_custom_call" | custom-call | flops 800000000 | bytes 4000000 | tf_op jit(solution)/shard_map/middle/pallas_call | solution.py:542
  34.7 0.0 copy-start
  34.7 26.7 %all_to_all.15.received = bf16[32,192,128]{2,1,0:T(8,128)(2,1)S(1)} all-to-all(bf16[32,192,128]{2,1,0:T(8,128)(2,1)S(1)} %middle.1), channel_id=1, replica_groups=mesh['illum'=8,'box'=32] {'box'}, dimensions={0} | all-to-all | bytes 3145728 | tf_op jit(solution)/shard_map/all_to_all | solution.py:562
  61.4 0.0 copy-done.1
  61.4 0.0 copy-done
  61.4 3.0 %down.1 = f32[2,16,128,128]{3,2,1,0:T(8,128)} custom-call(bf16[32,192,128]{2,1,0:T(8,128)(2,1)S(1)} %all_to_all.15.received, f32[2,2048,128]{2,1,0:T(8,128)S(1)} %copy-done, bf16[1024,1024]{1,0:T(8,128)(2,1)S(1)} %copy-done.1), custom_call_target="tpu_custom_call" | custom-call | flops 1200000000 | bytes 6000000 | tf_op jit(solution)/shard_map/down/pallas_call | solution.py:564
  (2 shorter events, 0.0 us)
Async XLA Ops:
  4.1 8.8 %copy-start.7 = (bf16[2,316,128]{2,0,1:T(2,128)(2,1)S(1)}, bf16[2,316,128]{2,0,1:T(2,128)(2,1)}, u32[]{:S(2)}) copy-start(bf16[2,316,128]{2,0,1:T(2,128)(2,1)} %param.17) | copy-start | bytes 485380
  4.1 9.5 %copy-start.6 = (bf16[2,316,512]{2,0,1:T(2,128)(2,1)S(1)}, bf16[2,316,512]{2,0,1:T(2,128)(2,1)}, u32[]{:S(2)}) copy-start(bf16[2,316,512]{2,0,1:T(2,128)(2,1)} %param.23) | copy-start | bytes 1941508
  4.1 10.4 %copy-start.4 = (s32[4]{0:T(128)S(1)}, s32[4]{0:T(128)}, u32[]{:S(2)}) copy-start(s32[4]{0:T(128)} %owner.3) | copy-start | bytes 52
  4.1 27.1 %all-to-all-start.1 = ((bf16[32,144,128]{2,1,0:T(8,128)(2,1)}), bf16[32,144,128]{2,1,0:T(8,128)(2,1)S(1)}, u32[]{:S(2)}, u32[]{:S(2)}) async-start(bf16[32,144,128]{2,1,0:T(8,128)(2,1)} %up.1), calls=%async_computation.1 | async-start | bytes 2359296 | tf_op jit(solution)/shard_map/all_to_all | solution.py:487
  25.0 6.9 %copy-start.2 = (bf16[16,64,128]{2,1,0:T(8,128)(2,1)S(1)}, bf16[16,64,128]{2,1,0:T(8,128)(2,1)}, u32[]{:S(2)}) copy-start(bf16[16,64,128]{2,1,0:T(8,128)(2,1)} %get-tuple-element.22.coupling) | copy-start | bytes 786436
  25.0 6.9 %copy-start.3 = (f32[2,3,8,128]{3,2,1,0:T(8,128)S(1)}, f32[2,3,8,128]{3,2,1,0:T(8,128)}, u32[]{:S(2)}) copy-start(f32[2,3,8,128]{3,2,1,0:T(8,128)} %get-tuple-element.23.table) | copy-start | bytes 73732
  25.1 6.9 %copy-start.5 = (s32[4]{0:T(128)S(1)}, s32[4]{0:T(128)}, u32[]{:S(2)}) copy-start(s32[4]{0:T(128)} %owner.3) | copy-start | bytes 52
  32.0 29.4 %copy-start.1 = (bf16[1024,1024]{1,0:T(8,128)(2,1)S(1)}, bf16[1024,1024]{1,0:T(8,128)(2,1)}, u32[]{:S(2)}) copy-start(bf16[1024,1024]{1,0:T(8,128)(2,1)} %get-tuple-element.25.weights) | copy-start | bytes 6291460
  34.7 26.7 %copy-start = (f32[2,2048,128]{2,1,0:T(8,128)S(1)}, f32[2,2048,128]{2,1,0:T(8,128)}, u32[]{:S(2)}) copy-start(f32[2,2048,128]{2,1,0:T(8,128)} %get-tuple-element.24.near) | copy-start | bytes 6291460
where the time goes:
time: 64.7 us; the launch traced here: 64.4 us
  blocking collectives  26.7 us (41%)
  Pallas kernels  19.6 us (30%)
  starting transfers between devices  8.73 us (13%)
  waiting for transfers between devices  6.16 us (10%)
  local copies, waits for them, and re-layouts  1.64 us (3%)
  between operations  0.82 us (1%)
  other arithmetic  0.77 us (1%)
    all_to_all x1, blocking collectives, shards(): lax.all_to_all(send, 'box', split_axis=0, concat_axis=0, tiled=True)  26.7 us
    pallas_call x1, Pallas kernels, shards(): pl.pallas_call(side_kernel, out_shape=made, in_specs=[SCALARS, *anywhere(...  9.76 us
    all_to_all x1, starting transfers between devices, shards(): lax.all_to_all(send, 'box', split_axis=0, concat_axis=0, tiled=True)  8.73 us
    all_to_all x1, waiting for transfers between devices, shards(): lax.all_to_all(send, 'box', split_axis=0, concat_axis=0, tiled=True)  6.16 us
    pallas_call x1, Pallas kernels, shards(): pl.pallas_call(up_kernel, out_shape=jax.ShapeDtypeStruct((DEV, SEND1, R),...  4.09 us
    pallas_call x1, Pallas kernels, shards(): pl.pallas_call(down_kernel, out_shape=jax.ShapeDtypeStruct((2, BOX, K, R)...  3.03 us
    pallas_call x1, Pallas kernels, shards(): pl.pallas_call(middle_kernel, out_shape=jax.ShapeDtypeStruct((DEV, SEND2,...  2.71 us
    unnamed x18, local copies, waits for them, and re-layouts  1.64 us
  transfers between devices with their start and end apart: 1, of which 1 were waited for; matrix products, arithmetic and copies ran while one was open for 4% of the time, Pallas kernels for 15%

commit v1 on v0

--- a/solution.py
+++ b/solution.py
@@ -121,8 +121,6 @@
             fields[rows : rows + K, (2 + p) * R : (3 + p) * R] = imag
             fields[rows + K : rows + 2 * K, (2 + p) * R : (3 + p) * R] = real
     first = first_parity(owner, me)
-    widen(patterns, wide, first)
-
     spread[:, 0 : index.shape[1]] = jnp.where(mask[...] > 0, index[...], NPAD - 1)
     lane = iota((BOX, LANES), 1)
     number = jnp.take_along_axis(
@@ -149,6 +147,8 @@
             preferred_element_type=F32,
         ).astype(BF16)
         here = range(t * ways, (t + 1) * ways)
+        if t == 0:
+            widen(patterns, wide, first)
         cut(send, L_ROWS, wide, here)
         for d in here:
             send[d, L_ROWS + P_ROWS : SEND1, :] = rows
@@ -378,13 +378,13 @@
         total = jnp.dot(left, right, preferred_element_type=F32)
         for c in range(2):
             for b in range(BOX):
-                moved[pl.ds((c * KS + k) * size + b, DEV, stride=BOX), :] = total[
+                moved[pl.ds((4 + c * KS + k) * size + b, DEV, stride=BOX), :] = total[
                     b * DEV : (b + 1) * DEV, c * R : (c + 1) * R
                 ]
     for ck in range(2 * KS):
         row = L_ROWS + ck * BOX
         send[:, row : row + BOX, :] = (
-            moved[ck * size : (ck + 1) * size, :].reshape(DEV, BOX, R).astype(BF16)
+            moved[(4 + ck) * size : (5 + ck) * size, :].reshape(DEV, BOX, R).astype(BF16)
         )
 
 
@@ -548,7 +548,7 @@
             pltpu.SemaphoreType.DMA((1,)),
             pltpu.VMEM((2, KS * FAR, R), F32),
             pltpu.VMEM((4 * size, R), F32),
-            pltpu.VMEM((2 * KS * size, R), F32),
+            pltpu.VMEM(((4 + 2 * KS) * size, R), F32),
             pltpu.VMEM((size, LANES), F32),
             pltpu.VMEM((16, R), BF16),
         ],

time: 64.7 us -> 64.7 us (level)
  no operation moved by 1% of the time
where the time goes in v1:
time: 64.7 us; the launch traced here: 64.4 us
  blocking collectives  26.7 us (41%)
  Pallas kernels  19.5 us (30%)
  starting transfers between devices  8.73 us (13%)
  waiting for transfers between devices  6.16 us (10%)
  local copies, waits for them, and re-layouts  1.64 us (3%)
  between operations  0.82 us (1%)
  other arithmetic  0.77 us (1%)
    all_to_all x1, blocking collectives, shards(): lax.all_to_all(send, 'box', split_axis=0, concat_axis=0, tiled=True)  26.7 us
    pallas_call x1, Pallas kernels, shards(): pl.pallas_call(side_kernel, out_shape=made, in_specs=[SCALARS, *anywhere(...  9.76 us
    all_to_all x1, starting transfers between devices, shards(): lax.all_to_all(send, 'box', split_axis=0, concat_axis=0, tiled=True)  8.73 us
    all_to_all x1, waiting for transfers between devices, shards(): lax.all_to_all(send, 'box', split_axis=0, concat_axis=0, tiled=True)  6.16 us
    pallas_call x1, Pallas kernels, shards(): pl.pallas_call(up_kernel, out_shape=jax.ShapeDtypeStruct((DEV, SEND1, R),...  4.09 us
    pallas_call x1, Pallas kernels, shards(): pl.pallas_call(down_kernel, out_shape=jax.ShapeDtypeStruct((2, BOX, K, R)...  3.03 us
    pallas_call x1, Pallas kernels, shards(): pl.pallas_call(middle_kernel, out_shape=jax.ShapeDtypeStruct((DEV, SEND2,...  2.65 us
    unnamed x18, local copies, waits for them, and re-layouts  1.64 us
  transfers between devices with their start and end apart: 1, of which 1 were waited for; matrix products, arithmetic and copies ran while one was open for 4% of the time, Pallas kernels for 15%

profile of v1, /device:TPU:1, one launch (start us, length us, event | category | flops | bytes accessed | tf_op | source)
XLA Modules:
  0.0 64.4 jit_solution(14344923433124154184)
XLA Ops:
  0.0 4.1 %up.1 = bf16[32,144,128]{2,1,0:T(8,128)(2,1)} custom-call(s32[4]{0:T(128)} %owner.3, bf16[2,16,128,128]{3,2,1,0:T(8,128)(2,1)} %patterns_in.3, s32[16,48]{1,0:T(8,128)} %index_in.3, s32[16,48]{1,0:T(8,128)} %mask_in.3, bf16[128,512]{1,0:T(8,128)(2,1)} %interp_in.3, f32[8,512]{1,0:T(8,128)} %angle_in.3), custom_call_target="tpu_custom_call" | custom-call | flops 1200000000 | bytes 4000000 | tf_op jit(solution)/shard_map/up/pallas_call | solution.py:460
  4.1 0.0 copy-start.7
  4.1 0.0 copy-start.6
  4.1 0.0 copy-start.4
  4.1 8.7 %all-to-all-start.1 = ((bf16[32,144,128]{2,1,0:T(8,128)(2,1)}), bf16[32,144,128]{2,1,0:T(8,128)(2,1)S(1)}, u32[]{:S(2)}, u32[]{:S(2)}) async-start(bf16[32,144,128]{2,1,0:T(8,128)(2,1)} %up.1), calls=%async_computation.1 | async-start | bytes 2359296 | tf_op jit(solution)/shard_map/all_to_all | solution.py:487
  12.9 0.0 copy-done.7
  12.9 0.7 %copy.14.table_in = bf16[2,316,128]{2,1,0:T(8,128)(2,1)} copy(bf16[2,316,128]{2,0,1:T(2,128)(2,1)S(1)} %copy-done.7) | data formatting | bytes 323584 | tf_op args[4]
  13.6 0.0 copy-done.6
  13.6 0.9 %copy.15.par_table_in = bf16[2,316,512]{2,1,0:T(8,128)(2,1)} copy(bf16[2,316,512]{2,0,1:T(2,128)(2,1)S(1)} %copy-done.6) | data formatting | bytes 1294336 | tf_op args[10]
  14.5 0.0 copy-done.4
  14.5 0.8 %and_reduce_fusion = pred[]{:T(512)} fusion(s32[4]{0:T(128)S(1)} %copy-done.4, s32[4]{0:T(128)S(1)} %broadcast_shift-right-arithmetic_fusion), kind=kLoop, calls=%fused_computation | loop fusion | flops 63 | bytes 33 | tf_op jit(solution)/shard_map/reduce_or | solution.py:532
  15.3 9.8 %side.1 = (f32[2,2048,128]{2,1,0:T(8,128)}, bf16[16,64,128]{2,1,0:T(8,128)(2,1)}, f32[2,3,8,128]{3,2,1,0:T(8,128)}, bf16[1024,1024]{1,0:T(8,128)(2,1)}, bf16[32,64,128]{2,1,0:T(8,128)(2,1)S(1)}) custom-call(s32[4]{0:T(128)} %owner.3, bf16[2,16,128,128]{3,2,1,0:T(8,128)(2,1)} %patterns_in.3, s32[16,48]{1,0:T(8,128)} %index_in.3, s32[16,48]{1,0:T(8,128)} %mask_in.3, ...), custom_call_target="tpu_custom_call" | custom-call | flops 4000000000 | bytes 12000000 | tf_op jit(solution)/shard_map/side/pallas_call | solution.py:497
  25.0 0.0 copy-start.2
  25.0 0.0 copy-start.3
  25.1 0.0 copy-start.5
  25.1 6.2 %all-to-all-done.1.received = bf16[32,144,128]{2,1,0:T(8,128)(2,1)S(1)} async-done(((bf16[32,144,128]{2,1,0:T(8,128)(2,1)}), bf16[32,144,128]{2,1,0:T(8,128)(2,1)S(1)}, u32[]{:S(2)}, u32[]{:S(2)}) %all-to-all-start.1) | async-done | bytes 1179680 | tf_op jit(solution)/shard_map/all_to_all | solution.py:487
  31.9 0.0 copy-done.2
  31.9 0.0 copy-done.3
  31.9 0.0 copy-done.5
  32.0 0.0 copy-start.1
  32.0 2.6 %middle.1 = bf16[32,192,128]{2,1,0:T(8,128)(2,1)S(1)} custom-call(s32[4]{0:T(128)S(1)} %copy-done.5, bf16[32,144,128]{2,1,0:T(8,128)(2,1)S(1)} %all-to-all-done.1.received, bf16[32,64,128]{2,1,0:T(8,128)(2,1)S(1)} %get-tuple-element.26.extra, bf16[16,64,128]{2,1,0:T(8,128)(2,1)S(1)} %copy-done.2, f32[2,3,8,128]{3,2,1,0:T(8,128)S(1)} %copy-done.3), custom_call_target="tpu_custom_call" | custom-call | flops 800000000 | bytes 4000000 | tf_op jit(solution)/shard_map/middle/pallas_call | solution.py:542
  34.6 0.0 copy-start
  34.6 26.7 %all_to_all.15.received = bf16[32,192,128]{2,1,0:T(8,128)(2,1)S(1)} all-to-all(bf16[32,192,128]{2,1,0:T(8,128)(2,1)S(1)} %middle.1), channel_id=1, replica_groups=mesh['illum'=8,'box'=32] {'box'}, dimensions={0} | all-to-all | bytes 3145728 | tf_op jit(solution)/shard_map/all_to_all | solution.py:562
  61.3 0.0 copy-done.1
  61.3 0.0 copy-done
  61.3 3.0 %down.1 = f32[2,16,128,128]{3,2,1,0:T(8,128)} custom-call(bf16[32,192,128]{2,1,0:T(8,128)(2,1)S(1)} %all_to_all.15.received, f32[2,2048,128]{2,1,0:T(8,128)S(1)} %copy-done, bf16[1024,1024]{1,0:T(8,128)(2,1)S(1)} %copy-done.1), custom_call_target="tpu_custom_call" | custom-call | flops 1200000000 | bytes 6000000 | tf_op jit(solution)/shard_map/down/pallas_call | solution.py:564
  (2 shorter events, 0.0 us)
Async XLA Ops:
  4.1 8.8 %copy-start.7 = (bf16[2,316,128]{2,0,1:T(2,128)(2,1)S(1)}, bf16[2,316,128]{2,0,1:T(2,128)(2,1)}, u32[]{:S(2)}) copy-start(bf16[2,316,128]{2,0,1:T(2,128)(2,1)} %param.17) | copy-start | bytes 485380
  4.1 9.5 %copy-start.6 = (bf16[2,316,512]{2,0,1:T(2,128)(2,1)S(1)}, bf16[2,316,512]{2,0,1:T(2,128)(2,1)}, u32[]{:S(2)}) copy-start(bf16[2,316,512]{2,0,1:T(2,128)(2,1)} %param.23) | copy-start | bytes 1941508
  4.1 10.4 %copy-start.4 = (s32[4]{0:T(128)S(1)}, s32[4]{0:T(128)}, u32[]{:S(2)}) copy-start(s32[4]{0:T(128)} %owner.3) | copy-start | bytes 52
  4.1 27.1 %all-to-all-start.1 = ((bf16[32,144,128]{2,1,0:T(8,128)(2,1)}), bf16[32,144,128]{2,1,0:T(8,128)(2,1)S(1)}, u32[]{:S(2)}, u32[]{:S(2)}) async-start(bf16[32,144,128]{2,1,0:T(8,128)(2,1)} %up.1), calls=%async_computation.1 | async-start | bytes 2359296 | tf_op jit(solution)/shard_map/all_to_all | solution.py:487
  25.0 6.9 %copy-start.2 = (bf16[16,64,128]{2,1,0:T(8,128)(2,1)S(1)}, bf16[16,64,128]{2,1,0:T(8,128)(2,1)}, u32[]{:S(2)}) copy-start(bf16[16,64,128]{2,1,0:T(8,128)(2,1)} %get-tuple-element.22.coupling) | copy-start | bytes 786436
  25.0 6.9 %copy-start.3 = (f32[2,3,8,128]{3,2,1,0:T(8,128)S(1)}, f32[2,3,8,128]{3,2,1,0:T(8,128)}, u32[]{:S(2)}) copy-start(f32[2,3,8,128]{3,2,1,0:T(8,128)} %get-tuple-element.23.table) | copy-start | bytes 73732
  25.1 6.9 %copy-start.5 = (s32[4]{0:T(128)S(1)}, s32[4]{0:T(128)}, u32[]{:S(2)}) copy-start(s32[4]{0:T(128)} %owner.3) | copy-start | bytes 52
  32.0 29.4 %copy-start.1 = (bf16[1024,1024]{1,0:T(8,128)(2,1)S(1)}, bf16[1024,1024]{1,0:T(8,128)(2,1)}, u32[]{:S(2)}) copy-start(bf16[1024,1024]{1,0:T(8,128)(2,1)} %get-tuple-element.25.weights) | copy-start | bytes 6291460
  34.6 26.7 %copy-start = (f32[2,2048,128]{2,1,0:T(8,128)S(1)}, f32[2,2048,128]{2,1,0:T(8,128)}, u32[]{:S(2)}) copy-start(f32[2,2048,128]{2,1,0:T(8,128)} %get-tuple-element.24.near) | copy-start | bytes 6291460
